TPU v7x, 1024 devices: a whole 4x4x32 slice. The times are simulated.
1024 devices in a mesh: diamond: 2 (over x_lo), tile: 512 (over y, z, x_hi, core).
Axes of the slice: x: 4 (x_hi: 2, x_lo: 2; x = x_hi * 2 + x_lo), y: 4, z: 32, core: 2. Of those that a mesh axis runs over, the one named last changes fastest.
Arguments:
- adjoint_temp: float32 [2, 512, 256, 128], P('diamond', 'tile'), may hold values from -6 to 6
- misfit: float32 [2, 512, 256, 128], P('diamond', 'tile'), may hold values from -4 to 4
- viscosity: float32 [2, 512, 256, 128], P('diamond', 'tile'), may hold values from 0.1 to 10
- velocity: float32 [3, 2, 512, 256, 128], P(None, 'diamond', 'tile'), may hold values from -6 to 6
- forcing: float32 [3, 2, 512, 256, 128], P(None, 'diamond', 'tile'), may hold values from -9 to 9
- edge_table: int32 [2, 256], replicated, may hold values from 0 to 255, as said below
- pole_table: int32 [2, 256], replicated, may hold values from 0 to 255, as said below
Outputs:
- solution: float32 [3, 2, 512, 256, 128], P(None, 'diamond', 'tile')
- residual: float32 [3, 2, 512, 256, 128], P(None, 'diamond', 'tile')
- adjoint_next: float32 [2, 512, 256, 128], P('diamond', 'tile')
Inputs may be any that keep to these rules, and one draw needn't show every extreme that they name: `edge_table`: each row of the table is a permutation of the 256 nodes, and row 1 is the inverse permutation of row 0. `pole_table`: each row of the table is a permutation of the 256 nodes, and row 1 is the inverse permutation of row 0.
All inputs are finite; a program needn't handle non-finite values.
Results may differ from a plain program's by a relative error of at most 0.008.
Values sent between devices are 32-bit elements; how exact they have to be, the bound alone decides.
A program may use at most 32 MiB of HBM per device.

v0:
```python
import jax
import jax.numpy as jnp
from jax import lax
from jax.sharding import PartitionSpec as P

ITERS = 3


TIME_STEP = 0.1
DIFFUSION = 1.0
MASS_TERM = 0.5
BUOYANCY = 1.0


def extended_2(shard, sides, width):
    for axis, dim in sides:
        size, length = (lax.axis_size(axis), shard.shape[dim])
        up = [(i, (i + 1) % size) for i in range(size - 1)]
        down = [(j, i) for i, j in up]
        last = lax.slice_in_dim(shard, length - width, length, axis=dim)
        leading = lax.slice_in_dim(shard, 0, width, axis=dim)
        before = lax.ppermute(last, axis, up)
        after = lax.ppermute(leading, axis, down)
        shard = jnp.concatenate([before, shard, after], axis=dim)
    return shard


def from_partner(value, axis, apart):
    mask = 2**apart
    pairs = [(source, source ^ mask) for source in range(lax.axis_size(axis))]
    return lax.ppermute(value, axis, pairs)


def outer_rows(field):
    return jnp.stack([field[:, :, 0], field[:, :, -1]], axis=2)


def assemble(field, extended, received, edge_table, pole_table):
    group = lax.axis_index("diamond")
    tile_index = lax.axis_index("tile")
    final = lax.axis_size("tile") - 1
    pole_line = lax.dynamic_index_in_dim(pole_table, group, 0, keepdims=False)
    edge_line = lax.dynamic_index_in_dim(edge_table, group, 0, keepdims=False)
    from_pole = jnp.take(received[:, :, 0], pole_line, axis=2)
    from_edge = jnp.take(received[:, :, 1], edge_line, axis=2)
    width = field.shape[2]
    first_row = jnp.where(tile_index == 0, from_pole, extended[:, :, 0])
    last_row = jnp.where(tile_index == final, from_edge, extended[:, :, width + 1])
    x_after = jnp.concatenate([extended[:, :, 2 : width + 1], last_row[:, :, None]], axis=2)
    x_before = jnp.concatenate([first_row[:, :, None], extended[:, :, 1:width]], axis=2)
    zeros_y = jnp.zeros_like(field[:, :, :, :1])
    y_after = jnp.concatenate([field[:, :, :, 1:], zeros_y], axis=3)
    y_before = jnp.concatenate([zeros_y, field[:, :, :, :-1]], axis=3)
    zeros_r = jnp.zeros_like(field[:, :, :, :, :1])
    r_after = jnp.concatenate([field[:, :, :, :, 1:], zeros_r], axis=4)
    r_before = jnp.concatenate([zeros_r, field[:, :, :, :, :-1]], axis=4)
    return [x_after, x_before, y_after, y_before, r_after, r_before]


def face_masks(count_y, count_r):
    y_place = jnp.arange(count_y)[:, None]
    r_place = jnp.arange(count_r)
    unity = jnp.ones((1, 1), jnp.float32)
    return [
        unity,
        unity,
        (y_place < count_y - 1).astype(jnp.float32),
        (y_place > 0).astype(jnp.float32),
        (r_place < count_r - 1).astype(jnp.float32),
        (r_place > 0).astype(jnp.float32),
    ]


def body(adjoint_temp, misfit, viscosity, velocity, forcing, edge_table, pole_table):
    paired = jnp.stack([adjoint_temp, viscosity])
    extended = extended_2(paired, (("tile", 2),), 1)
    received = from_partner(outer_rows(paired), "diamond", 0)
    near_both = assemble(paired, extended, received, edge_table, pole_table)
    temp_near = [entry[0] for entry in near_both]
    visc_near = [entry[1] for entry in near_both]
    laplace = sum(temp_near) - 6.0 * adjoint_temp
    transport = 0.5 * (
        velocity[0] * (temp_near[0] - temp_near[1])
        + velocity[1] * (temp_near[2] - temp_near[3])
        + velocity[2] * (temp_near[4] - temp_near[5])
    )
    adjoint_next = adjoint_temp + TIME_STEP * (DIFFUSION * laplace + transport) + misfit
    inside = face_masks(adjoint_temp.shape[2], adjoint_temp.shape[3])
    weights = [0.5 * (viscosity + visc_near[k]) * inside[k] for k in range(6)]
    diagonal = MASS_TERM + sum(weights)

    def combine(vector, near):
        total = diagonal * vector
        for k in range(6):
            total = total - weights[k] * near[k]
        return total

    def apply(vector):
        whole_ext = extended_2(vector, (("tile", 2),), 1)
        whole_got = from_partner(outer_rows(vector), "diamond", 0)
        near = assemble(vector, whole_ext, whole_got, edge_table, pole_table)
        return combine(vector, near)

    def products(residual, precond, image):
        return lax.psum(
            (jnp.sum(residual * precond), jnp.sum(precond * image)), ("diamond", "tile")
        )

    right = forcing.at[2].add(BUOYANCY * adjoint_next)
    solution = jnp.zeros_like(right)
    residual = right
    precond = residual / diagonal
    image = apply(precond)
    product_now, curvature = products(residual, precond, image)
    step_size = product_now / curvature
    direction, along = (precond, image)
    for step in range(ITERS):
        solution = solution + step_size * direction
        residual = residual - step_size * along
        if step + 1 < ITERS:
            precond = residual / diagonal
            image = apply(precond)
            product_next, curvature = products(residual, precond, image)
            ratio = product_next / product_now
            step_size = product_next / (curvature - ratio * product_next / step_size)
            direction = precond + ratio * direction
            along = image + ratio * along
            product_now = product_next
    return (solution, residual, adjoint_next)


def solution(mesh):
    placed = (
        P("diamond", "tile", None, None),
        P("diamond", "tile", None, None),
        P("diamond", "tile", None, None),
        P(None, "diamond", "tile", None, None),
        P(None, "diamond", "tile", None, None),
        P(),
        P(),
    )
    return jax.shard_map(
        body,
        mesh=mesh,
        in_specs=placed,
        out_specs=(
            P(None, "diamond", "tile", None, None),
            P(None, "diamond", "tile", None, None),
            P("diamond", "tile", None, None),
        ),
        check_vma=False,
    )
```

profile of v0, /device:TPU:1, one launch (start us, length us, event | category | flops | bytes accessed | tf_op | source)
XLA Modules:
  0.0 644.7 jit_solution(13361795866369941278)
XLA Ops:
  2.4 6.0 collective-permute-start.2
  8.4 12.0 %collective-permute-start.1 = (f32[2,1,1,256,128]{4,3,0,2,1:T(8,128)}, f32[2,1,1,256,128]{4,3,0,2,1:T(8,128)}, u32[]{:S(2)}, u32[]{:S(2)}) collective-permute-start(f32[2,1,1,256,128]{4,3,0,2,1:T(8,128)} %fusion.40), channel_id=1, source_target_pairs={{1,0},{2,1},{3,2},{4,3},{5,4},{6,5},{7,6},{8,7},{9,8},{10,9},{11,1... | collective-permute-start | bytes 786440 | tf_op jit(solution)/shard_map/ppermute | solution.py:23
  24.8 11.2 %collective-permute-done = f32[2,1,2,256,128]{4,3,2,1,0:T(8,128)S(1)} collective-permute-done((f32[2,1,2,256,128]{4,3,2,1,0:T(8,128)S(1)}, f32[2,1,2,256,128]{4,3,2,1,0:T(8,128)S(1)}, u32[]{:S(2)}, u32[]{:S(2)}) %collective-permute-start) | collective-permute-done | bytes 524320 | tf_op jit(solution)/shard_map/ppermute | solution.py:31
  41.5 2.9 scatter-add.4
  47.6 1.9 collective-permute-start.5
  49.6 3.2 collective-permute-start.4
  54.0 17.9 %collective-permute-done.3 = f32[3,1,2,256,128]{4,3,2,1,0:T(8,128)S(1)} collective-permute-done((f32[3,1,2,256,128]{4,3,2,1,0:T(8,128)S(1)}, f32[3,1,2,256,128]{4,3,2,1,0:T(8,128)S(1)}, u32[]{:S(2)}, u32[]{:S(2)}) %collective-permute-start.3) | collective-permute-done | bytes 786464 | tf_op jit(solution)/shard_map/ppermute | solution.py:31
  73.8 2.8 gather_fusion.2
  76.6 2.1 copy.123
  78.7 2.8 gather_fusion.3
  81.5 4.2 multiply_reduce_fusion.4
  85.7 162.2 %all-reduce.18 = (f32[]{:T(128)}, f32[]{:T(128)}) all-reduce(f32[]{:T(128)} %get-tuple-element.31, f32[]{:T(128)} %get-tuple-element.30), channel_id=1, replica_groups=mesh['diamond'=2,'tile'=512] {'diamond','tile'}, use_global_device_ids=true, to_apply=%region_1.3 | all-reduce | flops 2 | bytes 16 | tf_op jit(solution)/shard_map/psum | solution.py:105
  251.6 4.1 collective-permute-start.8
  255.7 1.9 collective-permute-start.7
  260.1 15.1 %collective-permute-done.6 = f32[3,1,2,256,128]{4,3,2,1,0:T(8,128)S(1)} collective-permute-done((f32[3,1,2,256,128]{4,3,2,1,0:T(8,128)S(1)}, f32[3,1,2,256,128]{4,3,2,1,0:T(8,128)S(1)}, u32[]{:S(2)}, u32[]{:S(2)}) %collective-permute-start.6) | collective-permute-done | bytes 786464 | tf_op jit(solution)/shard_map/ppermute | solution.py:31
  282.1 4.5 multiply_reduce_fusion.2
  286.6 151.8 %all-reduce.17 = (f32[]{:T(128)}, f32[]{:T(128)}) all-reduce(f32[]{:T(128)} %get-tuple-element.29, f32[]{:T(128)} %get-tuple-element.28), channel_id=1, replica_groups=mesh['diamond'=2,'tile'=512] {'diamond','tile'}, use_global_device_ids=true, to_apply=%region_5.8 | all-reduce | flops 2 | bytes 16 | tf_op jit(solution)/shard_map/psum | solution.py:105
  444.3 2.6 collective-permute-start.9
  446.9 5.2 collective-permute-start.11
  456.5 13.7 %collective-permute-done.9 = f32[3,1,2,256,128]{4,3,2,1,0:T(8,128)S(1)} collective-permute-done((f32[3,1,2,256,128]{4,3,2,1,0:T(8,128)S(1)}, f32[3,1,2,256,128]{4,3,2,1,0:T(8,128)S(1)}, u32[]{:S(2)}, u32[]{:S(2)}) %collective-permute-start.9) | collective-permute-done | bytes 786464 | tf_op jit(solution)/shard_map/ppermute | solution.py:31
  473.0 2.1 copy.119
  475.1 2.9 gather_fusion.7
  478.4 5.4 multiply_reduce_fusion
  483.8 154.2 %all-reduce.16 = (f32[]{:T(128)}, f32[]{:T(128)}) all-reduce(f32[]{:T(128)} %get-tuple-element.27, f32[]{:T(128)} %get-tuple-element.26), channel_id=1, replica_groups=mesh['diamond'=2,'tile'=512] {'diamond','tile'}, use_global_device_ids=true, to_apply=%region_9.12 | all-reduce | flops 2 | bytes 16 | tf_op jit(solution)/shard_map/psum | solution.py:105
  (98 shorter events, 41.2 us)
Async XLA Ops:
  0.6 19.8 %copy-start.1 = (f32[1,1,256,128]{3,2,1,0:T(8,128)S(1)}, f32[1,1,256,128]{3,2,1,0:T(8,128)}, u32[]{:S(2)}) copy-start(f32[1,1,256,128]{3,2,1,0:T(8,128)} %param.13) | copy-start | bytes 393220
  0.6 19.8 %copy-start.2 = (f32[1,1,256,128]{3,2,1,0:T(8,128)S(1)}, f32[1,1,256,128]{3,2,1,0:T(8,128)}, u32[]{:S(2)}) copy-start(f32[1,1,256,128]{3,2,1,0:T(8,128)} %param.15) | copy-start | bytes 393220
  2.4 36.1 %collective-permute-start.2 = (f32[2,1,1,256,128]{4,3,0,2,1:T(8,128)}, f32[2,1,1,256,128]{4,3,0,2,1:T(8,128)}, u32[]{:S(2)}, u32[]{:S(2)}) collective-permute-start(f32[2,1,1,256,128]{4,3,0,2,1:T(8,128)} %fusion.40), channel_id=1, source_target_pairs={{0,1},{1,2},{2,3},{3,4},{4,5},{5,6},{6,7},{7,8},{8,9},{9,10},{10,1... | collective-permute-start | bytes 786440 | tf_op jit(solution)/shard_map/ppermute | solution.py:22
  8.4 31.1 %collective-permute-start.1 = (f32[2,1,1,256,128]{4,3,0,2,1:T(8,128)}, f32[2,1,1,256,128]{4,3,0,2,1:T(8,128)}, u32[]{:S(2)}, u32[]{:S(2)}) collective-permute-start(f32[2,1,1,256,128]{4,3,0,2,1:T(8,128)} %fusion.40), channel_id=1, source_target_pairs={{1,0},{2,1},{3,2},{4,3},{5,4},{6,5},{7,6},{8,7},{9,8},{10,9},{11,1... | collective-permute-start | bytes 786440 | tf_op jit(solution)/shard_map/ppermute | solution.py:23
  20.5 15.5 %collective-permute-start = (f32[2,1,2,256,128]{4,3,2,1,0:T(8,128)S(1)}, f32[2,1,2,256,128]{4,3,2,1,0:T(8,128)S(1)}, u32[]{:S(2)}, u32[]{:S(2)}) collective-permute-start(f32[2,1,2,256,128]{4,3,2,1,0:T(8,128)S(1)} %maximum_maximum_fusion), channel_id=1, source_target_pairs={{0,512},{512,0},{1,513},{513,1},{2,514},{514,2},{3,515},{515,3},{4... | collective-permute-start | bytes 1572872 | tf_op jit(solution)/shard_map/ppermute | solution.py:31
  23.1 1.4 copy-start.8
  39.5 1.1 copy-start.9
  39.5 1.1 copy-start.10
  41.5 2.9 copy-start.12
  41.5 2.9 copy-start.14
  45.3 236.8 %copy-start.3 = (f32[256,128]{1,0:T(8,128)}, f32[256,128]{1,0:T(8,128)S(1)}, u32[]{:S(2)}) copy-start(f32[256,128]{1,0:T(8,128)S(1)} %get-tuple-element.70) | copy-start | bytes 393220
  45.3 236.8 %copy-start.4 = (f32[256,128]{1,0:T(8,128)}, f32[256,128]{1,0:T(8,128)S(1)}, u32[]{:S(2)}) copy-start(f32[256,128]{1,0:T(8,128)S(1)} %get-tuple-element.71) | copy-start | bytes 393220
  45.3 236.8 %copy-start.5 = (f32[256,128]{1,0:T(8,128)}, f32[256,128]{1,0:T(8,128)S(1)}, u32[]{:S(2)}) copy-start(f32[256,128]{1,0:T(8,128)S(1)} %get-tuple-element.72) | copy-start | bytes 393220
  45.3 236.8 %copy-start.6 = (f32[256,128]{1,0:T(8,128)}, f32[256,128]{1,0:T(8,128)S(1)}, u32[]{:S(2)}) copy-start(f32[256,128]{1,0:T(8,128)S(1)} %get-tuple-element.73) | copy-start | bytes 393220
  45.7 26.2 %collective-permute-start.3 = (f32[3,1,2,256,128]{4,3,2,1,0:T(8,128)S(1)}, f32[3,1,2,256,128]{4,3,2,1,0:T(8,128)S(1)}, u32[]{:S(2)}, u32[]{:S(2)}) collective-permute-start(f32[3,1,2,256,128]{4,3,2,1,0:T(8,128)S(1)} %copy.94), channel_id=1, source_target_pairs={{0,512},{512,0},{1,513},{513,1},{2,514},{514,2},{3,515},{515,3},{4... | collective-permute-start | bytes 2359304 | tf_op jit(solution)/shard_map/ppermute | solution.py:31
  47.6 33.9 %collective-permute-start.5 = (f32[3,1,1,256,128]{4,0,3,2,1:T(4,128)S(1)}, f32[3,1,1,256,128]{4,0,3,2,1:T(4,128)}, u32[]{:S(2)}, u32[]{:S(2)}) collective-permute-start(f32[3,1,1,256,128]{4,0,3,2,1:T(4,128)S(1)} %broadcast_divide_fusion.2), channel_id=1, source_target_pairs={{0,1},{1,2},{2,3},{3,4},{4,5},{5,6},{6,7},{7,8},{8,9},{9,10},{10,1... | collective-permute-start | bytes 1179656 | tf_op jit(solution)/shard_map/ppermute | solution.py:22
  49.6 31.9 %collective-permute-start.4 = (f32[3,1,1,256,128]{4,0,3,2,1:T(4,128)S(1)}, f32[3,1,1,256,128]{4,0,3,2,1:T(4,128)}, u32[]{:S(2)}, u32[]{:S(2)}) collective-permute-start(f32[3,1,1,256,128]{4,0,3,2,1:T(4,128)S(1)} %broadcast_divide_fusion.2), channel_id=1, source_target_pairs={{1,0},{2,1},{3,2},{4,3},{5,4},{6,5},{7,6},{8,7},{9,8},{10,9},{11,1... | collective-permute-start | bytes 1179656 | tf_op jit(solution)/shard_map/ppermute | solution.py:23
  249.7 25.5 %collective-permute-start.6 = (f32[3,1,2,256,128]{4,3,2,1,0:T(8,128)S(1)}, f32[3,1,2,256,128]{4,3,2,1,0:T(8,128)S(1)}, u32[]{:S(2)}, u32[]{:S(2)}) collective-permute-start(f32[3,1,2,256,128]{4,3,2,1,0:T(8,128)S(1)} %copy.97), channel_id=1, source_target_pairs={{0,512},{512,0},{1,513},{513,1},{2,514},{514,2},{3,515},{515,3},{4... | collective-permute-start | bytes 2359304 | tf_op jit(solution)/shard_map/ppermute | solution.py:31
  251.6 29.4 %collective-permute-start.8 = (f32[3,1,1,256,128]{4,0,3,2,1:T(4,128)S(1)}, f32[3,1,1,256,128]{4,0,3,2,1:T(4,128)}, u32[]{:S(2)}, u32[]{:S(2)}) collective-permute-start(f32[3,1,1,256,128]{4,0,3,2,1:T(4,128)S(1)} %get-tuple-element.42), channel_id=1, source_target_pairs={{0,1},{1,2},{2,3},{3,4},{4,5},{5,6},{6,7},{7,8},{8,9},{9,10},{10,1... | collective-permute-start | bytes 1179656 | tf_op jit(solution)/shard_map/ppermute | solution.py:22
  255.7 26.4 %collective-permute-start.7 = (f32[3,1,1,256,128]{4,0,3,2,1:T(4,128)S(1)}, f32[3,1,1,256,128]{4,0,3,2,1:T(4,128)}, u32[]{:S(2)}, u32[]{:S(2)}) collective-permute-start(f32[3,1,1,256,128]{4,0,3,2,1:T(4,128)S(1)} %get-tuple-element.42), channel_id=1, source_target_pairs={{1,0},{2,1},{3,2},{4,3},{5,4},{6,5},{7,6},{8,7},{9,8},{10,9},{11,1... | collective-permute-start | bytes 1179656 | tf_op jit(solution)/shard_map/ppermute | solution.py:23
  444.3 25.9 %collective-permute-start.9 = (f32[3,1,2,256,128]{4,3,2,1,0:T(8,128)S(1)}, f32[3,1,2,256,128]{4,3,2,1,0:T(8,128)S(1)}, u32[]{:S(2)}, u32[]{:S(2)}) collective-permute-start(f32[3,1,2,256,128]{4,3,2,1,0:T(8,128)S(1)} %copy.100), channel_id=1, source_target_pairs={{0,512},{512,0},{1,513},{513,1},{2,514},{514,2},{3,515},{515,3},{4... | collective-permute-start | bytes 2359304 | tf_op jit(solution)/shard_map/ppermute | solution.py:31
  446.9 31.0 %collective-permute-start.11 = (f32[3,1,1,256,128]{4,0,3,2,1:T(4,128)S(1)}, f32[3,1,1,256,128]{4,0,3,2,1:T(4,128)}, u32[]{:S(2)}, u32[]{:S(2)}) collective-permute-start(f32[3,1,1,256,128]{4,0,3,2,1:T(4,128)S(1)} %get-tuple-element.39), channel_id=1, source_target_pairs={{0,1},{1,2},{2,3},{3,4},{4,5},{5,6},{6,7},{7,8},{8,9},{9,10},{10,1... | collective-permute-start | bytes 1179656 | tf_op jit(solution)/shard_map/ppermute | solution.py:22
  452.1 26.4 %collective-permute-start.10 = (f32[3,1,1,256,128]{4,0,3,2,1:T(4,128)S(1)}, f32[3,1,1,256,128]{4,0,3,2,1:T(4,128)}, u32[]{:S(2)}, u32[]{:S(2)}) collective-permute-start(f32[3,1,1,256,128]{4,0,3,2,1:T(4,128)S(1)} %get-tuple-element.39), channel_id=1, source_target_pairs={{1,0},{2,1},{3,2},{4,3},{5,4},{6,5},{7,6},{8,7},{9,8},{10,9},{11,1... | collective-permute-start | bytes 1179656 | tf_op jit(solution)/shard_map/ppermute | solution.py:23
  475.1 3.4 copy-start
  (5 other events, 3.9 us)
where the time goes:
time: 646 us; the launch traced here: 645 us
  blocking collectives  468 us (72%)
  waiting for transfers between devices  59.4 us (9%)
  starting transfers between devices  44.6 us (7%)
  local copies, waits for them, and re-layouts  38.7 us (6%)
  other arithmetic  22.9 us (4%)
  between operations  10.9 us (2%)
    psum x3, blocking collectives, products(): lax.psum((jnp.sum(residual * precond), jnp.sum(precond * image)), ('diamo...  468 us
    ppermute x4, waiting for transfers between devices, from_partner(): return lax.ppermute(value, axis, pairs)  57.9 us
    ppermute x4, starting transfers between devices, extended_2(): after = lax.ppermute(leading, axis, down)  19 us
    ppermute x4, starting transfers between devices, extended_2(): before = lax.ppermute(last, axis, up)  17.2 us
    reduce_sum x3, other arithmetic, products(): jnp.sum(precond * image)  14.1 us
  transfers between devices with their start and end apart: 12, of which 6 were waited for; matrix products, arithmetic and copies ran while one was open for 5% of the time, Pallas kernels for 0%

commit v1 on v0

v1 whole, which is shorter than its diff:
```python
import functools

import jax
import jax.numpy as jnp
from jax import lax
from jax.experimental import pallas as pl
from jax.experimental.pallas import tpu as pltpu
from jax.sharding import PartitionSpec as P

ITERS = 3
TIME_STEP = 0.1
DIFFUSION = 1.0
MASS_TERM = 0.5
BUOYANCY = 1.0

NY = 256
NR = 128
COMPS = 3
MOMENTS = 2 * ITERS
MESH = pl.DeviceIdType.MESH
NX_CHIPS = 4
NY_CHIPS = 4
NZ_CHIPS = 32
Z_ROUNDS = 4


def device_at(x, y, z, core):
    return (lax.rem(x, 2), ((y * NZ_CHIPS + z) * 2 + x // 2) * 2 + core)


def shift(value, step, axis):
    return pltpu.roll(value, (-step) % value.shape[axis], axis)


def total_of(value):
    return jnp.sum(jnp.sum(value, axis=0, keepdims=True), axis=1, keepdims=True)


def lane_row(entries):
    lane = lax.broadcasted_iota(jnp.int32, (1, NR), 1)
    row = jnp.zeros((1, NR), jnp.float32)
    for k, entry in enumerate(entries):
        row = row + jnp.where(lane == k, entry, 0.0)
    return row


def gradient_coefficients(mu):
    def inner(left, right):
        result = None
        for i, a in enumerate(left):
            for j, b in enumerate(right):
                term = a * b * mu[i + j]
                result = term if result is None else result + term
        return result

    one, zero = jnp.ones_like(mu[0]), jnp.zeros_like(mu[0])
    place, rest, direction = [zero] * ITERS, [one] + [zero] * ITERS, [one]
    now = mu[0]
    for step in range(ITERS):
        image = [direction[0]]
        for i in range(1, len(direction)):
            image.append(direction[i] - direction[i - 1])
        image.append(-direction[-1])
        size = now / inner(direction, image)
        for i, entry in enumerate(direction):
            place[i] = place[i] + size * entry
        for i, entry in enumerate(image):
            rest[i] = rest[i] - size * entry
        if step + 1 < ITERS:
            part = rest[: step + 2]
            later = inner(part, part)
            ratio = later / now
            direction = [part[i] + (ratio * direction[i] if i < len(direction) else 0.0) for i in range(len(part))]
            now = later
    return place, rest


def kernel(
    last,
    temp_in, misfit_in, visc_in, vel_in, forc_in, edge_in, pole_in,
    sol_out, res_out, adj_out,
    temp, misfit, visc, vel, forc, tables, halo0, halo, vs, weights, diag, adj, sol, onehot,
    xbuf, ybuf, zbuf, cbuf, mine,
    load_sem, store_sem, send0, recv0, send, recv, small_send, small_recv, know,
):
    group = lax.axis_index("diamond")
    tile = lax.axis_index("tile")
    core = lax.rem(tile, 2)
    x = lax.rem(tile // 2, 2) * 2 + group
    z = lax.rem(tile // 4, NZ_CHIPS)
    y = tile // (4 * NZ_CHIPS)
    first, final = tile == 0, tile == last

    before_dev = (jnp.where(first, 1 - group, group), jnp.where(first, 0, tile - 1))
    after_dev = (jnp.where(final, 1 - group, group), jnp.where(final, last, tile + 1))
    side_dev = (before_dev, after_dev)
    side_slot = (jnp.where(first, 0, 1), jnp.where(final, 1, 0))

    def x_dev(i):
        return device_at(x ^ i, y, z, core)

    def y_dev(i):
        return device_at(x, y ^ i, z, core)

    def z_dev(i):
        return device_at(x, y, lax.rem(z + i + NZ_CHIPS, NZ_CHIPS), core)

    loads = [
        pltpu.make_async_copy(source, target, load_sem.at[i])
        for i, (source, target) in enumerate(
            ((visc_in, visc), (temp_in, temp), (forc_in, forc), (misfit_in, misfit), (vel_in, vel), (edge_in, tables.at[1]), (pole_in, tables.at[0]))
        )
    ]
    for load in loads:
        load.start()

    barrier = pltpu.get_barrier_semaphore()
    greeted = [*side_dev, x_dev(1), x_dev(3), y_dev(1), y_dev(3), z_dev(-1), z_dev(1)]
    for dev in greeted:
        pl.semaphore_signal(barrier, inc=1, device_id=dev, device_id_type=MESH)
    pl.semaphore_wait(barrier, len(greeted))

    def first_copy(side, k):
        return pltpu.make_async_remote_copy(
            src_ref=(visc_in, temp_in)[k],
            dst_ref=halo0.at[side_slot[side], k],
            send_sem=send0.at[side, k],
            recv_sem=recv0.at[side_slot[side], k],
            device_id=side_dev[side],
            device_id_type=MESH,
        )

    def first_arrival(side, k):
        pltpu.make_async_remote_copy(
            src_ref=halo0.at[side, k],
            dst_ref=halo0.at[side, k],
            send_sem=send0.at[side, k],
            recv_sem=recv0.at[side, k],
            device_id=side_dev[side],
            device_id_type=MESH,
        ).wait_recv()

    def row_copy(step, side, c):
        return pltpu.make_async_remote_copy(
            src_ref=vs.at[step, c],
            dst_ref=halo.at[step, side_slot[side], c],
            send_sem=send.at[step, side, c],
            recv_sem=recv.at[step, side_slot[side], c],
            device_id=side_dev[side],
            device_id_type=MESH,
        )

    def row_arrival(step, side, c):
        pltpu.make_async_remote_copy(
            src_ref=halo.at[step, side, c],
            dst_ref=halo.at[step, side, c],
            send_sem=send.at[step, side, c],
            recv_sem=recv.at[step, side, c],
            device_id=side_dev[side],
            device_id_type=MESH,
        ).wait_recv()

    def reorder(ref, side):
        @pl.when((first, final)[side])
        def _():
            ref[...] = jnp.dot(onehot[...], ref[...], precision=lax.Precision.HIGHEST, preferred_element_type=jnp.float32)

    for k in range(2):
        for side in range(2):
            first_copy(side, k).start()

    def tell(round_, devs):
        for dev in devs:
            pl.semaphore_signal(know.at[round_], inc=1, device_id=dev, device_id_type=MESH)

    def hear(round_):
        pl.semaphore_wait(know.at[round_], 2)

    tell(0, (z_dev(-1), z_dev(1)))
    tell(Z_ROUNDS, (x_dev(1), x_dev(3)))
    tell(Z_ROUNDS + 1, (y_dev(1), y_dev(3)))

    loads[5].wait()
    loads[6].wait()

    for side in range(2):

        @pl.when((first, final)[side])
        def _():
            inverse = jnp.where(group == 0, tables[side, 1:2, :], tables[side, 0:1, :])
            place = lax.broadcasted_iota(jnp.int32, (NY, NY), 0)
            onehot[...] = jnp.where(place == inverse, 1.0, 0.0).astype(jnp.float32)

    y_place = lax.broadcasted_iota(jnp.int32, (NY, NR), 0)
    r_place = lax.broadcasted_iota(jnp.int32, (NY, NR), 1)
    inside = (y_place < NY - 1, y_place > 0, r_place < NR - 1, r_place > 0)
    moves = ((1, 0), (-1, 0), (1, 1), (-1, 1))

    loads[0].wait()
    own = visc[...]
    rowwise = MASS_TERM
    for k, (step, axis) in enumerate(moves):
        weight = jnp.where(inside[k], 0.5 * (own + shift(own, step, axis)), 0.0)
        weights[2 + k] = weight
        rowwise = rowwise + weight
    diag[...] = rowwise

    for side in range(2):
        first_arrival(side, 0)
        reorder(halo0.at[side, 0], side)
    after = 0.5 * (visc[...] + halo0[1, 0])
    before = 0.5 * (visc[...] + halo0[0, 0])
    diagonal = diag[...] + after + before
    diag[...] = diagonal
    inverse_diagonal = 1.0 / diagonal
    weights[0] = after * inverse_diagonal
    weights[1] = before * inverse_diagonal
    for k in range(2, 6):
        weights[k] = weights[k] * inverse_diagonal

    loads[2].wait()
    for c in range(COMPS - 1):
        vs[0, c] = forc[c] / diag[...]
        for side in range(2):
            row_copy(0, side, c).start()

    loads[1].wait()
    loads[3].wait()
    loads[4].wait()
    own = temp[...]
    near = [jnp.where(inside[k], shift(own, step, axis), 0.0) for k, (step, axis) in enumerate(moves)]
    rowwise = own + misfit[...] + TIME_STEP * (
        DIFFUSION * (near[0] + near[1] + near[2] + near[3] - 6.0 * own)
        + 0.5 * (vel[1] * (near[0] - near[1]) + vel[2] * (near[2] - near[3]))
    )
    adj[...] = rowwise
    for side in range(2):
        first_arrival(side, 1)
        reorder(halo0.at[side, 1], side)
    after, before = halo0[1, 1], halo0[0, 1]
    adj[...] = adj[...] + TIME_STEP * (DIFFUSION * (after + before) + 0.5 * (vel[0] * (after - before)))
    vs[0, COMPS - 1] = (forc[COMPS - 1] + BUOYANCY * adj[...]) / diag[...]
    for side in range(2):
        row_copy(0, side, COMPS - 1).start()
    adj_store = pltpu.make_async_copy(adj, adj_out, store_sem.at[2])
    adj_store.start()

    hear(0)
    tell(1, (z_dev(-2), z_dev(2)))

    def in_row(step, c):
        value = vs[step, c]
        result = None
        for k, (move, axis) in enumerate(moves):
            term = weights[2 + k] * shift(value, move, axis)
            result = term if result is None else result + term
        vs[step + 1, c] = result

    mu = []
    for step in range(ITERS - 1):
        for c in range(COMPS):
            in_row(step, c)
        even = diag[...] * sum(vs[step, c] * vs[step, c] for c in range(COMPS))
        mu.append(total_of(even))
        for c in range(COMPS):
            for side in range(2):
                row_arrival(step, side, c)
                reorder(halo.at[step, side, c], side)
            vs[step + 1, c] = vs[step + 1, c] + weights[0] * halo[step, 1, c] + weights[1] * halo[step, 0, c]
            row_copy(step + 1, 1, c).start()
            if step + 2 < ITERS:
                row_copy(step + 1, 0, c).start()
            else:

                @pl.when(first)
                def _():
                    row_copy(step + 1, 0, c).start()

        odd = diag[...] * sum(vs[step, c] * vs[step + 1, c] for c in range(COMPS))
        mu.append(total_of(odd))
        hear(1 + step)
        tell(2 + step, (z_dev(-(4 << step)), z_dev(4 << step)))
        if step == 0:
            hear(Z_ROUNDS)
            hear(Z_ROUNDS + 1)

    step = ITERS - 1
    for c in range(COMPS):
        in_row(step, c)
    mu.append(total_of(diag[...] * sum(vs[step, c] * vs[step, c] for c in range(COMPS))))
    inner_part = sum(vs[step, c] * vs[step + 1, c] for c in range(COMPS))
    edges = None
    for c in range(COMPS):
        row_arrival(step, 0, c)
        reorder(halo.at[step, 0, c], 0)
        part = weights[1] * halo[step, 0, c]
        vs[step + 1, c] = vs[step + 1, c] + part
        term = vs[step, c] * part
        edges = term if edges is None else edges + term
    count = jnp.where(first, 1.0, 2.0)
    mu.append(total_of(diag[...] * (inner_part + count * edges)))
    mine[...] = lane_row(mu)

    @pl.when(final)
    def _():
        edges = None
        for c in range(COMPS):
            row_arrival(step, 1, c)
            reorder(halo.at[step, 1, c], 1)
            term = vs[step, c] * halo[step, 1, c]
            edges = term if edges is None else edges + term
        mine[...] = mine[...] + lane_row([0.0] * (MOMENTS - 1) + [total_of(diag[...] * weights[0] * edges)])

    def small_copy(i, buffer, slot, dev):
        return pltpu.make_async_remote_copy(
            src_ref=mine, dst_ref=buffer.at[slot], send_sem=small_send.at[i], recv_sem=small_recv.at[i], device_id=dev, device_id_type=MESH
        )

    def spread(i, buffer, slot, devs):
        buffer[slot] = mine[...]
        for dev in devs:
            small_copy(i, buffer, slot, dev).start()

    def gather(i, buffer, count):
        shape = buffer.at[pl.ds(0, count)]
        whole = pltpu.make_async_remote_copy(
            src_ref=shape, dst_ref=shape, send_sem=small_send.at[i], recv_sem=small_recv.at[i], device_id=x_dev(1), device_id_type=MESH
        )
        whole.wait_send()
        whole.wait_recv()
        mine[...] = jnp.sum(buffer[...], axis=0)

    spread(0, cbuf, core, [device_at(x, y, z, 1 - core)])
    gather(0, cbuf, 1)
    spread(1, xbuf, x, [x_dev(2), x_dev(1), x_dev(3)])
    gather(1, xbuf, NX_CHIPS - 1)
    spread(2, ybuf, y, [y_dev(2), y_dev(1), y_dev(3)])
    gather(2, ybuf, NY_CHIPS - 1)
    hear(Z_ROUNDS - 1)
    zbuf[z] = mine[...]

    def z_send(i, carry):
        k = (i + 1) // 2
        offset = NZ_CHIPS // 2 + k * (1 - 2 * lax.rem(i, 2))
        small_copy(3, zbuf, z, z_dev(offset)).start()
        return carry

    lax.fori_loop(0, NZ_CHIPS - 1, z_send, 0)

    for c in range(COMPS):

        @pl.when(jnp.logical_not(first))
        def _():
            row_copy(step, 0, c).start()

    for c in range(COMPS):

        @pl.when(jnp.logical_not(final))
        def _():
            row_arrival(step, 1, c)

        vs[step + 1, c] = vs[step + 1, c] + weights[0] * halo[step, 1, c]

    gather(3, zbuf, NZ_CHIPS - 1)
    sums = mine[...]
    place, rest = gradient_coefficients([sums[:, k : k + 1] for k in range(MOMENTS)])
    for c in range(COMPS):
        sol[0, c] = sum(place[k] * vs[k, c] for k in range(ITERS))
    sol_store = pltpu.make_async_copy(sol.at[0], sol_out, store_sem.at[0])
    sol_store.start()
    for c in range(COMPS):
        sol[1, c] = diag[...] * sum(rest[k] * vs[k, c] for k in range(ITERS + 1))
    res_store = pltpu.make_async_copy(sol.at[1], res_out, store_sem.at[1])
    res_store.start()

    for k in range(2):
        for side in range(2):
            first_copy(side, k).wait_send()
    for s in range(ITERS):
        for side in range(2):
            for c in range(COMPS):
                row_copy(s, side, c).wait_send()
    adj_store.wait()
    sol_store.wait()
    res_store.wait()


def body(adjoint_temp, misfit, viscosity, velocity, forcing, edge_table, pole_table):
    row = (NY, NR)
    rows = (COMPS, NY, NR)
    f32 = jnp.float32
    any_space = pl.BlockSpec(memory_space=pl.ANY)
    sol, res, adj = pl.pallas_call(
        functools.partial(kernel, lax.axis_size("tile") - 1),
        out_shape=(
            jax.ShapeDtypeStruct(rows, f32),
            jax.ShapeDtypeStruct(rows, f32),
            jax.ShapeDtypeStruct(row, f32),
        ),
        in_specs=[any_space] * 7,
        out_specs=(any_space,) * 3,
        scratch_shapes=[
            pltpu.VMEM(row, f32),
            pltpu.VMEM(row, f32),
            pltpu.VMEM(row, f32),
            pltpu.VMEM(rows, f32),
            pltpu.VMEM(rows, f32),
            pltpu.VMEM((2, 2, NY), jnp.int32),
            pltpu.VMEM((2, 2, *row), f32),
            pltpu.VMEM((ITERS, 2, *rows), f32),
            pltpu.VMEM((ITERS + 1, *rows), f32),
            pltpu.VMEM((6, *row), f32),
            pltpu.VMEM(row, f32),
            pltpu.VMEM(row, f32),
            pltpu.VMEM((2, *rows), f32),
            pltpu.VMEM((NY, NY), f32),
            pltpu.VMEM((NX_CHIPS, 1, NR), f32),
            pltpu.VMEM((NY_CHIPS, 1, NR), f32),
            pltpu.VMEM((NZ_CHIPS, 1, NR), f32),
            pltpu.VMEM((2, 1, NR), f32),
            pltpu.VMEM((1, NR), f32),
            pltpu.SemaphoreType.DMA((7,)),
            pltpu.SemaphoreType.DMA((3,)),
            pltpu.SemaphoreType.DMA((2, 2)),
            pltpu.SemaphoreType.DMA((2, 2)),
            pltpu.SemaphoreType.DMA((ITERS, 2, COMPS)),
            pltpu.SemaphoreType.DMA((ITERS, 2, COMPS)),
            pltpu.SemaphoreType.DMA((4,)),
            pltpu.SemaphoreType.DMA((4,)),
            pltpu.SemaphoreType.REGULAR((Z_ROUNDS + 2,)),
        ],
        compiler_params=pltpu.CompilerParams(collective_id=0, has_side_effects=True, vmem_limit_bytes=32 << 20),
    )(
        adjoint_temp.reshape(row),
        misfit.reshape(row),
        viscosity.reshape(row),
        velocity.reshape(rows),
        forcing.reshape(rows),
        edge_table,
        pole_table,
    )
    shape = adjoint_temp.shape
    return sol.reshape((COMPS, *shape)), res.reshape((COMPS, *shape)), adj.reshape(shape)


def solution(mesh):
    placed = (
        P("diamond", "tile", None, None),
        P("diamond", "tile", None, None),
        P("diamond", "tile", None, None),
        P(None, "diamond", "tile", None, None),
        P(None, "diamond", "tile", None, None),
        P(),
        P(),
    )
    return jax.shard_map(
        body,
        mesh=mesh,
        in_specs=placed,
        out_specs=(
            P(None, "diamond", "tile", None, None),
            P(None, "diamond", "tile", None, None),
            P("diamond", "tile", None, None),
        ),
        check_vma=False,
    )
```

time: 646 us -> 86.5 us (0.13)
  blocking collectives: 468 us -> 0 us
  Pallas kernels: 0 us -> 77.2 us
  waiting for transfers between devices: 59.4 us -> 0 us
  starting transfers between devices: 44.6 us -> 0 us
  local copies, waits for them, and re-layouts: 38.7 us -> 7.53 us
  other arithmetic: 22.9 us -> 0 us
  between operations: 10.9 us -> 0.66 us
    psum x3 -> x0, blocking collectives: 468 us -> none  [products(): lax.psum((jnp.sum(residual * precond), jnp.sum(precond * image)), ('diamo...]
    pallas_call x0 -> x1, Pallas kernels: none -> 77.2 us  [body(): pl.pallas_call(functools.partial(kernel, lax.axis_size('tile') - 1), out_...]
    ppermute x12 -> x0, waiting for transfers between devices: 59.4 us -> none  [the longest x4 57.9 us: from_partner(): return lax.ppermute(value, axis, pairs)]
    ppermute x12 -> x0, starting transfers between devices: 44.6 us -> none  [the longest x4 19 us: extended_2(): after = lax.ppermute(leading, axis, down)]
    gather x8 -> x0, local copies, waits for them, and re-layouts: 15.7 us -> none  [the longest x4 8.4 us: assemble(): from_pole = jnp.take(received[:, :, 0], pole_line, axis=2)]
    reduce_sum x3 -> x0, other arithmetic: 14.1 us -> none  [products(): jnp.sum(precond * image)]
    slice x9 -> x0, local copies, waits for them, and re-layouts: 8.62 us -> none  [the longest x3 3.16 us: assemble(): y_after = jnp.concatenate([field[:, :, :, 1:], zeros_y], axis=3)]
  transfers between devices with their start and end apart: 12 -> 0, of which waited for: 6 -> 0; matrix products, arithmetic and copies ran while one was open for 5% -> 0% of each run, Pallas kernels for 0% -> 0%
where the time goes in v1:
time: 86.5 us; the launch traced here: 85.4 us
  Pallas kernels  77.2 us (89%)
  local copies, waits for them, and re-layouts  7.53 us (9%)
    pallas_call x1, Pallas kernels, body(): pl.pallas_call(functools.partial(kernel, lax.axis_size('tile') - 1), out_...  77.2 us
    unnamed x17, local copies, waits for them, and re-layouts  7.53 us

profile of v1, /device:TPU:1, one launch (start us, length us, event | category | flops | bytes accessed | tf_op | source)
XLA Modules:
  0.0 85.4 jit_solution(13741145115413314221)
XLA Ops:
  0.6 0.0 copy-start.6
  0.6 0.0 copy-start.5
  0.7 0.7 copy-done.6
  1.3 0.0 copy-done.5
  1.3 0.0 copy-start
  1.3 1.0 %copy-done = f32[3,1,1,256,128]{4,3,2,1,0:T(8,128)S(1)} copy-done((f32[3,1,1,256,128]{4,3,2,1,0:T(8,128)S(1)}, f32[3,1,1,256,128]{4,3,2,1,0:T(8,128)}, u32[]{:S(2)}) %copy-start) | copy-done | bytes 393240
  2.3 0.0 copy-start.1
  2.3 1.0 %copy-done.1 = f32[3,1,1,256,128]{4,3,2,1,0:T(8,128)S(1)} copy-done((f32[3,1,1,256,128]{4,3,2,1,0:T(8,128)S(1)}, f32[3,1,1,256,128]{4,3,2,1,0:T(8,128)}, u32[]{:S(2)}) %copy-start.1) | copy-done | bytes 393240
  3.3 0.0 copy-start.2
  3.3 0.9 %copy-done.2 = f32[1,1,256,128]{3,2,1,0:T(8,128)S(1)} copy-done((f32[1,1,256,128]{3,2,1,0:T(8,128)S(1)}, f32[1,1,256,128]{3,2,1,0:T(8,128)}, u32[]{:S(2)}) %copy-start.2) | copy-done | bytes 131096
  4.2 0.0 copy-start.3
  4.2 0.9 %copy-done.3 = f32[1,1,256,128]{3,2,1,0:T(8,128)S(1)} copy-done((f32[1,1,256,128]{3,2,1,0:T(8,128)S(1)}, f32[1,1,256,128]{3,2,1,0:T(8,128)}, u32[]{:S(2)}) %copy-start.3) | copy-done | bytes 131096
  5.1 0.0 copy-start.4
  5.1 0.9 %copy-done.4 = f32[1,1,256,128]{3,2,1,0:T(8,128)S(1)} copy-done((f32[1,1,256,128]{3,2,1,0:T(8,128)S(1)}, f32[1,1,256,128]{3,2,1,0:T(8,128)}, u32[]{:S(2)}) %copy-start.4) | copy-done | bytes 131096
  6.0 77.2 %shard_map.94 = (f32[3,256,128]{2,1,0:T(8,128)S(1)}, f32[3,256,128]{2,1,0:T(8,128)S(1)}, f32[256,128]{1,0:T(8,128)S(1)}) custom-call(f32[256,128]{1,0:T(8,128)S(1)} %bitcast.16, f32[256,128]{1,0:T(8,128)S(1)} %bitcast.17, f32[256,128]{1,0:T(8,128)S(1)} %bitcast.18, f32[3,256,128]{2,1,0:T(8,128)S(1)} %bitcast.14, f32[3,256,128]{2,1,0:T(8,128)S(1)} %bitcast.15, ...), custom_call_target="tpu_custom_call" | custom-call | tf_op jit(solution)/shard_map/pallas_call | solution.py:393
  83.2 0.7 copy.15
  84.0 0.7 copy.16
  84.7 0.7 copy.17
Async XLA Ops:
  0.6 0.7 copy-start.6
  0.6 0.7 copy-start.5
  1.3 1.0 %copy-start = (f32[3,1,1,256,128]{4,3,2,1,0:T(8,128)S(1)}, f32[3,1,1,256,128]{4,3,2,1,0:T(8,128)}, u32[]{:S(2)}) copy-start(f32[3,1,1,256,128]{4,3,2,1,0:T(8,128)} %param.10) | copy-start | bytes 1179652
  2.3 1.0 %copy-start.1 = (f32[3,1,1,256,128]{4,3,2,1,0:T(8,128)S(1)}, f32[3,1,1,256,128]{4,3,2,1,0:T(8,128)}, u32[]{:S(2)}) copy-start(f32[3,1,1,256,128]{4,3,2,1,0:T(8,128)} %param.11) | copy-start | bytes 1179652
  3.3 0.9 %copy-start.2 = (f32[1,1,256,128]{3,2,1,0:T(8,128)S(1)}, f32[1,1,256,128]{3,2,1,0:T(8,128)}, u32[]{:S(2)}) copy-start(f32[1,1,256,128]{3,2,1,0:T(8,128)} %param.7) | copy-start | bytes 393220
  4.2 0.9 %copy-start.3 = (f32[1,1,256,128]{3,2,1,0:T(8,128)S(1)}, f32[1,1,256,128]{3,2,1,0:T(8,128)}, u32[]{:S(2)}) copy-start(f32[1,1,256,128]{3,2,1,0:T(8,128)} %param.8) | copy-start | bytes 393220
  5.1 0.9 %copy-start.4 = (f32[1,1,256,128]{3,2,1,0:T(8,128)S(1)}, f32[1,1,256,128]{3,2,1,0:T(8,128)}, u32[]{:S(2)}) copy-start(f32[1,1,256,128]{3,2,1,0:T(8,128)} %param.9) | copy-start | bytes 393220

commit v2 on v1

v2 whole, which is shorter than its diff:
```python
import functools

import jax
import jax.numpy as jnp
from jax import lax
from jax.experimental import pallas as pl
from jax.experimental.pallas import tpu as pltpu
from jax.sharding import PartitionSpec as P

ITERS = 3
TIME_STEP = 0.1
DIFFUSION = 1.0
MASS_TERM = 0.5
BUOYANCY = 1.0

NY = 256
NR = 128
HALF = NY // 2
COMPS = 3
MOMENTS = 2 * ITERS
MESH = pl.DeviceIdType.MESH
NX_CHIPS = 4
NY_CHIPS = 4
NZ_CHIPS = 32
Z_ROUNDS = 4


def device_at(x, y, z, core):
    return (lax.rem(x, 2), ((y * NZ_CHIPS + z) * 2 + x // 2) * 2 + core)


def shift(value, step, axis):
    return pltpu.roll(value, (-step) % value.shape[axis], axis)


def total_of(value):
    return jnp.sum(jnp.sum(value[0] + value[1], axis=0, keepdims=True), axis=1, keepdims=True)


def lane_row(entries):
    lane = lax.broadcasted_iota(jnp.int32, (1, NR), 1)
    row = jnp.zeros((1, NR), jnp.float32)
    for k, entry in enumerate(entries):
        row = row + jnp.where(lane == k, entry, 0.0)
    return row


def gradient_coefficients(mu):
    def inner(left, right):
        result = None
        for i, a in enumerate(left):
            for j, b in enumerate(right):
                term = a * b * mu[i + j]
                result = term if result is None else result + term
        return result

    one, zero = jnp.ones_like(mu[0]), jnp.zeros_like(mu[0])
    place, rest, direction = [zero] * ITERS, [one] + [zero] * ITERS, [one]
    now = mu[0]
    for step in range(ITERS):
        image = [direction[0]]
        for i in range(1, len(direction)):
            image.append(direction[i] - direction[i - 1])
        image.append(-direction[-1])
        size = now / inner(direction, image)
        for i, entry in enumerate(direction):
            place[i] = place[i] + size * entry
        for i, entry in enumerate(image):
            rest[i] = rest[i] - size * entry
        if step + 1 < ITERS:
            part = rest[: step + 2]
            later = inner(part, part)
            ratio = later / now
            direction = [part[i] + (ratio * direction[i] if i < len(direction) else 0.0) for i in range(len(part))]
            now = later
    return place, rest


def kernel(
    last,
    temp_in, misfit_in, visc_in, vel_in, forc_in, edge_in, pole_in,
    sol_out, res_out, adj_out,
    temp, misfit, vel, forc, tables, beside, moved, near, partner, line_out, line_in, vs, weights, far, diag, adj, right, home, sol, onehot,
    xbuf, ybuf, zbuf, cbuf, mine,
    load_sem, store_sem, temp_send, temp_recv, move_send, move_recv, move_own, in_send, in_recv, out_send, out_recv, line_send, line_recv,
    back_send, back_recv, small_send, small_recv, know,
):
    group = lax.axis_index("diamond")
    tile = lax.axis_index("tile")
    core = lax.rem(tile, 2)
    half = lax.rem(tile // 2, 2)
    quad = tile // 4
    x = half * 2 + group
    z = lax.rem(quad, NZ_CHIPS)
    y = quad // NZ_CHIPS
    first, final = tile == 0, tile == last
    opens = jnp.logical_and(quad == 0, core == 0)
    closes = jnp.logical_and(quad == last // 4, core == 1)
    at_end = jnp.logical_or(opens, closes)
    within = jnp.logical_not(at_end)
    outer_home = core == half

    def quad_dev(which_half, which_core):
        return (group, quad * 4 + which_half * 2 + which_core)

    def partner_dev(which_half):
        return (1 - group, quad * 4 + which_half * 2 + core)

    def x_dev(i):
        return device_at(x ^ i, y, z, core)

    def y_dev(i):
        return device_at(x, y ^ i, z, core)

    def z_dev(i):
        return device_at(x, y, lax.rem(z + i + NZ_CHIPS, NZ_CHIPS), core)

    inner_dev = quad_dev(half, 1 - core)
    outer_dev = (group, jnp.where(at_end, tile, jnp.where(core == 0, tile - 3, tile + 3)))
    line_dev = quad_dev(1 - half, core)
    before_dev = (jnp.where(first, 1 - group, group), jnp.where(first, 0, tile - 1))
    after_dev = (jnp.where(final, 1 - group, group), jnp.where(final, last, tile + 1))
    side_dev = (before_dev, after_dev)
    side_slot = (jnp.where(first, 0, 1), jnp.where(final, 1, 0))
    here = pl.ds(pl.multiple_of(half * HALF, HALF), HALF)

    loads = [
        pltpu.make_async_copy(source, target, load_sem.at[i])
        for i, (source, target) in enumerate(
            ((temp_in, temp), (misfit_in, misfit), (vel_in, vel), (forc_in, forc), (edge_in, tables.at[1]), (pole_in, tables.at[0]))
        )
    ]
    for load in loads:
        load.start()

    barrier = pltpu.get_barrier_semaphore()

    def greet(dev):
        pl.semaphore_signal(barrier, inc=1, device_id=dev, device_id_type=MESH)

    greeted = [inner_dev, line_dev, quad_dev(1 - half, 1 - core), x_dev(1), x_dev(3), y_dev(1), y_dev(3), z_dev(-1), z_dev(1)]
    for dev in greeted:
        greet(dev)
    home_beside = jnp.logical_and(outer_home, within)

    @pl.when(within)
    def _():
        greet(outer_dev)

    @pl.when(home_beside)
    def _():
        greet((group, jnp.where(core == 0, tile - 1, tile + 1)))

    @pl.when(at_end)
    def _():
        greet(partner_dev(0))
        greet(partner_dev(1))

    pl.semaphore_wait(barrier, len(greeted) + jnp.where(at_end, 2, jnp.where(home_beside, 2, 1)))

    def remote(source, target, send_sem, recv_sem, dev):
        return pltpu.make_async_remote_copy(
            src_ref=source, dst_ref=target, send_sem=send_sem, recv_sem=recv_sem, device_id=dev, device_id_type=MESH
        )

    def arrived(target, recv_sem):
        remote(target, target, temp_send.at[0], recv_sem, inner_dev).wait_recv()

    def temp_copy(side):
        return remote(temp_in, beside.at[side_slot[side]], temp_send.at[side], temp_recv.at[side_slot[side]], side_dev[side])

    sources = [visc_in, forc_in.at[0], forc_in.at[1], right]
    slot = jnp.where(outer_home, 0, 1)

    def move_copy(f, h):
        return remote(sources[f].at[pl.ds(h * HALF, HALF)], moved.at[f, slot], move_send.at[f, h], move_recv.at[f, slot], quad_dev(h, half))

    def own_copy(f):
        return pltpu.make_async_copy(sources[f].at[here], moved.at[f, 0], move_own.at[f])

    def move(f):
        for h in range(2):

            @pl.when(jnp.logical_not(jnp.logical_and(outer_home, half == h)))
            def _():
                move_copy(f, h).start()

        @pl.when(outer_home)
        def _():
            own_copy(f).start()

    def move_sent(f):
        for h in range(2):

            @pl.when(jnp.logical_not(jnp.logical_and(outer_home, half == h)))
            def _():
                move_copy(f, h).wait_send()

    def move_done(f):
        @pl.when(outer_home)
        def _():
            own_copy(f).wait()

        @pl.when(jnp.logical_not(outer_home))
        def _():
            arrived(moved.at[f, 0], move_recv.at[f, 0])

        arrived(moved.at[f, 1], move_recv.at[f, 1])

    def in_copy(s, c, rows):
        return remote(rows.at[1], near.at[s, c, 1], in_send.at[s, c], in_recv.at[s, c], inner_dev)

    def out_copy(s, c, rows):
        return remote(rows.at[0], near.at[s, c, 0], out_send.at[s, c, 0], out_recv.at[s, c, 0], outer_dev)

    def end_copy(s, c, rows, h):
        return remote(rows.at[0], partner.at[s, c, here], out_send.at[s, c, h], out_recv.at[s, c, half], partner_dev(h))

    def line_copy(s, c):
        return remote(line_out.at[s, c], line_in.at[s, c], line_send.at[s, c], line_recv.at[s, c], line_dev)

    def give(s, c, rows):
        @pl.when(within)
        def _():
            out_copy(s, c, rows).start()

        @pl.when(at_end)
        def _():
            for h in range(2):
                end_copy(s, c, rows, h).start()

        line_out[s, c] = jnp.where(half == 0, rows[:, HALF - 1 : HALF, :], rows[:, 0:1, :])
        line_copy(s, c).start()
        in_copy(s, c, rows).start()

    def given(s, c, rows):
        @pl.when(within)
        def _():
            out_copy(s, c, rows).wait_send()

        @pl.when(at_end)
        def _():
            for h in range(2):
                end_copy(s, c, rows, h).wait_send()

        line_copy(s, c).wait_send()
        in_copy(s, c, rows).wait_send()

    def take(s, c):
        arrived(near.at[s, c, 1], in_recv.at[s, c])
        arrived(line_in.at[s, c], line_recv.at[s, c])

        @pl.when(within)
        def _():
            arrived(near.at[s, c, 0], out_recv.at[s, c, 0])

        @pl.when(at_end)
        def _():
            for h in range(2):
                arrived(partner.at[s, c, pl.ds(h * HALF, HALF)], out_recv.at[s, c, h])
            near[s, c, 0] = jnp.dot(
                onehot[here, :], partner[s, c], precision=lax.Precision.HIGHEST, preferred_element_type=jnp.float32
            )

    def back_copy(a, rows, p):
        return remote(
            rows.at[p], home.at[a, here], back_send.at[a, p], back_recv.at[a, half], quad_dev(core, (core, 1 - core)[p])
        )

    def give_back(a, rows):
        @pl.when(outer_home)
        def _():
            home[a, here, :] = rows[0]

        @pl.when(jnp.logical_not(outer_home))
        def _():
            back_copy(a, rows, 0).start()

        back_copy(a, rows, 1).start()

    def back_sent(a, rows):
        @pl.when(jnp.logical_not(outer_home))
        def _():
            back_copy(a, rows, 0).wait_send()

        back_copy(a, rows, 1).wait_send()

    def back_done(a):
        for h in range(2):

            @pl.when(jnp.logical_not(jnp.logical_and(outer_home, half == h)))
            def _():
                arrived(home.at[a, pl.ds(h * HALF, HALF)], back_recv.at[a, h])

    for side in range(2):
        temp_copy(side).start()
    for f in range(3):
        move(f)

    def tell(round_, devs):
        for dev in devs:
            pl.semaphore_signal(know.at[round_], inc=1, device_id=dev, device_id_type=MESH)

    def hear(round_):
        pl.semaphore_wait(know.at[round_], 2)

    tell(0, (z_dev(-1), z_dev(1)))
    tell(Z_ROUNDS, (x_dev(1), x_dev(3)))
    tell(Z_ROUNDS + 1, (y_dev(1), y_dev(3)))

    loads[4].wait()
    loads[5].wait()

    for at, end in enumerate((opens, closes)):

        @pl.when(end)
        def _():
            inverse = jnp.where(group == 0, tables[at, 1:2, :], tables[at, 0:1, :])
            place = lax.broadcasted_iota(jnp.int32, (NY, NY), 0)
            onehot[...] = jnp.where(place == inverse, 1.0, 0.0).astype(jnp.float32)

    for load in loads[:4]:
        load.wait()
    y_place = lax.broadcasted_iota(jnp.int32, (NY, NR), 0)
    r_place = lax.broadcasted_iota(jnp.int32, (NY, NR), 1)
    inside = (y_place < NY - 1, y_place > 0, r_place < NR - 1, r_place > 0)
    own = temp[...]
    other = [jnp.where(inside[k], shift(own, step, axis), 0.0) for k, (step, axis) in enumerate(((1, 0), (-1, 0), (1, 1), (-1, 1)))]
    adj[...] = own + misfit[...] + TIME_STEP * (
        DIFFUSION * (other[0] + other[1] + other[2] + other[3] - 6.0 * own)
        + 0.5 * (vel[1] * (other[0] - other[1]) + vel[2] * (other[2] - other[3]))
    )
    for side in range(2):
        arrived(beside.at[side], temp_recv.at[side])

        @pl.when((first, final)[side])
        def _():
            beside[side] = jnp.dot(onehot[...], beside[side], precision=lax.Precision.HIGHEST, preferred_element_type=jnp.float32)

    after, before = beside[1], beside[0]
    adj[...] = adj[...] + TIME_STEP * (DIFFUSION * (after + before) + 0.5 * (vel[0] * (after - before)))
    right[...] = forc[COMPS - 1] + BUOYANCY * adj[...]
    move(3)
    adj_store = pltpu.make_async_copy(adj, adj_out, store_sem.at[2])
    adj_store.start()
    hear(0)
    tell(1, (z_dev(-2), z_dev(2)))

    moves = ((1, 1), (-1, 1), (1, 2), (-1, 2))
    shape = (2, HALF, NR)
    y_place = lax.broadcasted_iota(jnp.int32, shape, 1)
    r_place = lax.broadcasted_iota(jnp.int32, shape, 2)
    inside = (y_place < HALF - 1, y_place > 0, r_place < NR - 1, r_place > 0)
    move_done(0)
    visc = moved.at[0]
    give(ITERS, 0, visc)
    own = visc[...]
    local = jnp.full(shape, MASS_TERM, jnp.float32)
    for k, (step, axis) in enumerate(moves):
        weight = jnp.where(inside[k], 0.5 * (own + shift(own, step, axis)), 0.0)
        weights[k] = weight
        local = local + weight
    between = 0.5 * (own[0] + own[1])
    for p in range(2):
        weights[4, p] = between
    diag[...] = local + weights[4]
    take(ITERS, 0)
    border = line_in[ITERS, 0]
    for at, (place, own_half) in enumerate(((HALF - 1, 0), (0, 1))):
        rows = slice(place, place + 1)
        weight = jnp.where(half == own_half, 0.5 * (visc[:, rows, :] + border), 0.0)
        diag[:, rows, :] = diag[:, rows, :] + weight
        far[at] = weight
    outside = 0.5 * (visc[...] + near[ITERS, 0])
    diagonal = diag[...] + outside
    diag[...] = diagonal
    inverse_diagonal = 1.0 / diagonal
    weights[5] = outside * inverse_diagonal
    for k in range(5):
        weights[k] = weights[k] * inverse_diagonal
    for at, place in enumerate((HALF - 1, 0)):
        far[at] = far[at] * inverse_diagonal[:, place : place + 1, :]

    for c in range(COMPS):
        move_done(1 + c)
        vs[0, c] = moved[1 + c] / diag[...]
        give(0, c, vs.at[0, c])

    mu = []
    for step in range(ITERS):
        for c in range(COMPS):
            value = vs[step, c]
            result = weights[4, 0] * value[1], weights[4, 1] * value[0]
            vs[step + 1, c, 0] = result[0]
            vs[step + 1, c, 1] = result[1]
            part = vs[step + 1, c]
            for k, (move_by, axis) in enumerate(moves):
                part = part + weights[k] * shift(value, move_by, axis)
            vs[step + 1, c] = part
        mu.append(total_of(diag[...] * sum(vs[step, c] * vs[step, c] for c in range(COMPS))))
        for c in range(COMPS):
            take(step, c)
            vs[step + 1, c] = vs[step + 1, c] + weights[5] * near[step, c]
            for at, place in enumerate((HALF - 1, 0)):
                rows = slice(place, place + 1)
                vs[step + 1, c, :, rows, :] = vs[step + 1, c, :, rows, :] + far[at] * line_in[step, c]
            if step + 1 < ITERS:
                give(step + 1, c, vs.at[step + 1, c])
        mu.append(total_of(diag[...] * sum(vs[step, c] * vs[step + 1, c] for c in range(COMPS))))
        if step + 1 < ITERS:
            if step == 0:
                give_back(0, diag)
                hear(Z_ROUNDS)
                hear(Z_ROUNDS + 1)
            for c in range(COMPS):
                give_back(1 + step * COMPS + c, vs.at[step + 1, c])
            hear(1 + step)
            tell(2 + step, (z_dev(-(4 << step)), z_dev(4 << step)))

    def small_copy(i, buffer, slot, dev):
        return remote(mine, buffer.at[slot], small_send.at[i], small_recv.at[i], dev)

    def spread(i, buffer, slot, devs):
        buffer[slot] = mine[...]
        for dev in devs:
            small_copy(i, buffer, slot, dev).start()

    def gather(i, buffer, count):
        part = buffer.at[pl.ds(0, count)]
        whole = remote(part, part, small_send.at[i], small_recv.at[i], inner_dev)
        whole.wait_send()
        whole.wait_recv()
        mine[...] = jnp.sum(buffer[...], axis=0)

    mine[...] = lane_row(mu)
    hear(Z_ROUNDS - 1)
    zbuf[z] = mine[...]

    def z_send(i, carry):
        k = (i + 1) // 2
        offset = NZ_CHIPS // 2 + k * (1 - 2 * lax.rem(i, 2))
        small_copy(3, zbuf, z, z_dev(offset)).start()
        return carry

    lax.fori_loop(0, NZ_CHIPS - 1, z_send, 0)
    for c in range(COMPS):
        give_back(1 + (ITERS - 1) * COMPS + c, vs.at[ITERS, c])
    gather(3, zbuf, NZ_CHIPS - 1)
    spread(0, cbuf, core, [inner_dev])
    gather(0, cbuf, 1)
    spread(1, xbuf, x, [x_dev(2), x_dev(1), x_dev(3)])
    gather(1, xbuf, NX_CHIPS - 1)
    spread(2, ybuf, y, [y_dev(2), y_dev(1), y_dev(3)])
    for a in range(1 + ITERS * COMPS):
        back_done(a)
    gather(2, ybuf, NY_CHIPS - 1)
    sums = mine[...]
    place, rest = gradient_coefficients([sums[:, k : k + 1] for k in range(MOMENTS)])
    for c in range(COMPS):
        full = forc[c] if c + 1 < COMPS else right[...]
        krylov = [full / home[0]] + [home[1 + step * COMPS + c] for step in range(ITERS)]
        sol[0, c] = sum(place[k] * krylov[k] for k in range(ITERS))
        sol[1, c] = rest[0] * full + home[0] * sum(rest[k] * krylov[k] for k in range(1, ITERS + 1))
    sol_store = pltpu.make_async_copy(sol.at[0], sol_out, store_sem.at[0])
    sol_store.start()
    res_store = pltpu.make_async_copy(sol.at[1], res_out, store_sem.at[1])
    res_store.start()

    for side in range(2):
        temp_copy(side).wait_send()
    for f in range(1 + COMPS):
        move_sent(f)
    given(ITERS, 0, visc)
    back_sent(0, diag)
    for s in range(ITERS):
        for c in range(COMPS):
            given(s, c, vs.at[s, c])
            back_sent(1 + s * COMPS + c, vs.at[s + 1, c])
    adj_store.wait()
    sol_store.wait()
    res_store.wait()


def body(adjoint_temp, misfit, viscosity, velocity, forcing, edge_table, pole_table):
    row = (NY, NR)
    rows = (COMPS, NY, NR)
    pair = (2, HALF, NR)
    f32 = jnp.float32
    dma = pltpu.SemaphoreType.DMA
    any_space = pl.BlockSpec(memory_space=pl.ANY)
    sol, res, adj = pl.pallas_call(
        functools.partial(kernel, lax.axis_size("tile") - 1),
        out_shape=(
            jax.ShapeDtypeStruct(rows, f32),
            jax.ShapeDtypeStruct(rows, f32),
            jax.ShapeDtypeStruct(row, f32),
        ),
        in_specs=[any_space] * 7,
        out_specs=(any_space,) * 3,
        scratch_shapes=[
            pltpu.VMEM(row, f32),
            pltpu.VMEM(row, f32),
            pltpu.VMEM(rows, f32),
            pltpu.VMEM(rows, f32),
            pltpu.VMEM((2, 2, NY), jnp.int32),
            pltpu.VMEM((2, *row), f32),
            pltpu.VMEM((1 + COMPS, *pair), f32),
            pltpu.VMEM((ITERS + 1, COMPS, *pair), f32),
            pltpu.VMEM((ITERS + 1, COMPS, *row), f32),
            pltpu.VMEM((ITERS + 1, COMPS, 2, 1, NR), f32),
            pltpu.VMEM((ITERS + 1, COMPS, 2, 1, NR), f32),
            pltpu.VMEM((ITERS + 1, COMPS, *pair), f32),
            pltpu.VMEM((6, *pair), f32),
            pltpu.VMEM((2, 2, 1, NR), f32),
            pltpu.VMEM(pair, f32),
            pltpu.VMEM(row, f32),
            pltpu.VMEM(row, f32),
            pltpu.VMEM((1 + ITERS * COMPS, *row), f32),
            pltpu.VMEM((2, *rows), f32),
            pltpu.VMEM((NY, NY), f32),
            pltpu.VMEM((NX_CHIPS, 1, NR), f32),
            pltpu.VMEM((NY_CHIPS, 1, NR), f32),
            pltpu.VMEM((NZ_CHIPS, 1, NR), f32),
            pltpu.VMEM((2, 1, NR), f32),
            pltpu.VMEM((1, NR), f32),
            dma((6,)),
            dma((3,)),
            dma((2,)),
            dma((2,)),
            dma((1 + COMPS, 2)),
            dma((1 + COMPS, 2)),
            dma((1 + COMPS,)),
            dma((ITERS + 1, COMPS)),
            dma((ITERS + 1, COMPS)),
            dma((ITERS + 1, COMPS, 2)),
            dma((ITERS + 1, COMPS, 2)),
            dma((ITERS + 1, COMPS)),
            dma((ITERS + 1, COMPS)),
            dma((1 + ITERS * COMPS, 2)),
            dma((1 + ITERS * COMPS, 2)),
            dma((4,)),
            dma((4,)),
            pltpu.SemaphoreType.REGULAR((Z_ROUNDS + 2,)),
        ],
        compiler_params=pltpu.CompilerParams(collective_id=0, has_side_effects=True, vmem_limit_bytes=60 << 20),
    )(
        adjoint_temp.reshape(row),
        misfit.reshape(row),
        viscosity.reshape(row),
        velocity.reshape(rows),
        forcing.reshape(rows),
        edge_table,
        pole_table,
    )
    shape = adjoint_temp.shape
    return sol.reshape((COMPS, *shape)), res.reshape((COMPS, *shape)), adj.reshape(shape)


def solution(mesh):
    placed = (
        P("diamond", "tile", None, None),
        P("diamond", "tile", None, None),
        P("diamond", "tile", None, None),
        P(None, "diamond", "tile", None, None),
        P(None, "diamond", "tile", None, None),
        P(),
        P(),
    )
    return jax.shard_map(
        body,
        mesh=mesh,
        in_specs=placed,
        out_specs=(
            P(None, "diamond", "tile", None, None),
            P(None, "diamond", "tile", None, None),
            P("diamond", "tile", None, None),
        ),
        check_vma=False,
    )
```

time: 86.5 us -> 75.3 us (0.87)
  Pallas kernels: 77.2 us -> 70 us
  local copies, waits for them, and re-layouts: 7.53 us -> 3.5 us
    pallas_call x1, Pallas kernels: 77.2 us -> 70 us  [body(): pl.pallas_call(functools.partial(kernel, lax.axis_size('tile') - 1), out_...]
    unnamed x17 -> x7, local copies, waits for them, and re-layouts: 7.53 us -> 3.5 us
where the time goes in v2:
time: 75.3 us; the launch traced here: 74.2 us
  Pallas kernels  70 us (93%)
  local copies, waits for them, and re-layouts  3.5 us (5%)
    pallas_call x1, Pallas kernels, body(): pl.pallas_call(functools.partial(kernel, lax.axis_size('tile') - 1), out_...  70 us
    unnamed x7, local copies, waits for them, and re-layouts  3.5 us

profile of v2, /device:TPU:1, one launch (start us, length us, event | category | flops | bytes accessed | tf_op | source)
XLA Modules:
  0.0 74.2 jit_solution(9453947696272518175)
XLA Ops:
  0.6 70.0 %shard_map.94 = (f32[3,256,128]{2,1,0:T(8,128)}, f32[3,256,128]{2,1,0:T(8,128)}, f32[256,128]{1,0:T(8,128)}) custom-call(f32[256,128]{1,0:T(8,128)} %bitcast.16, f32[256,128]{1,0:T(8,128)} %bitcast.17, f32[256,128]{1,0:T(8,128)} %bitcast.18, f32[3,256,128]{2,1,0:T(8,128)} %bitcast.14, f32[3,256,128]{2,1,0:T(8,128)} %bitcast.15, s32[2,256]{1,0:T(2,128)} %edge_in.1, ...), custom_call_target="tpu_custom_call" | custom-call | tf_op jit(solution)/shard_map/pallas_call | solution.py:491
  70.7 0.0 copy-start
  70.7 1.8 %copy.15 = f32[3,1,1,256,128]{4,3,2,1,0:T(8,128)} copy(f32[3,1,1,256,128]{4,3,2,1,0:T(8,128)} %bitcast.13) | data formatting | bytes 786432
  72.5 0.0 copy-done
  72.5 0.0 copy-start.1
  72.5 0.7 %copy.16 = f32[3,1,1,256,128]{4,3,2,1,0:T(8,128)} copy(f32[3,1,1,256,128]{4,3,2,1,0:T(8,128)S(1)} %bitcast.12) | data formatting | bytes 786432
  73.2 0.3 copy-done.1
  73.5 0.7 copy.17
Async XLA Ops:
  70.7 1.8 %copy-start = (f32[3,256,128]{2,1,0:T(8,128)S(1)}, f32[3,256,128]{2,1,0:T(8,128)}, u32[]{:S(2)}) copy-start(f32[3,256,128]{2,1,0:T(8,128)} %get-tuple-element.7) | copy-start | bytes 1179652
  72.5 1.0 %copy-start.1 = (f32[256,128]{1,0:T(8,128)S(1)}, f32[256,128]{1,0:T(8,128)}, u32[]{:S(2)}) copy-start(f32[256,128]{1,0:T(8,128)} %get-tuple-element.8) | copy-start | bytes 393220

commit v3 on v2

--- a/solution.py
+++ b/solution.py
@@ -16,6 +16,8 @@
 NY = 256
 NR = 128
 HALF = NY // 2
+SPARE = 8
+HELD = HALF + SPARE
 COMPS = 3
 MOMENTS = 2 * ITERS
 MESH = pl.DeviceIdType.MESH
@@ -23,6 +25,7 @@
 NY_CHIPS = 4
 NZ_CHIPS = 32
 Z_ROUNDS = 4
+PLANE = NX_CHIPS * NY_CHIPS * 2
 
 
 def device_at(x, y, z, core):
@@ -80,9 +83,9 @@
     last,
     temp_in, misfit_in, visc_in, vel_in, forc_in, edge_in, pole_in,
     sol_out, res_out, adj_out,
-    temp, misfit, vel, forc, tables, beside, moved, near, partner, line_out, line_in, vs, weights, far, diag, adj, right, home, sol, onehot,
-    xbuf, ybuf, zbuf, cbuf, mine,
-    load_sem, store_sem, temp_send, temp_recv, move_send, move_recv, move_own, in_send, in_recv, out_send, out_recv, line_send, line_recv,
+    temp, misfit, vel, forc, tables, beside, moved, near, partner, vs, weights, diag, measure, adj, right, home, sol, onehot,
+    zbuf, plane, mine,
+    load_sem, store_sem, temp_send, temp_recv, move_send, move_recv, move_own, in_send, in_recv, out_send, out_recv,
     back_send, back_recv, small_send, small_recv, know,
 ):
     group = lax.axis_index("diamond")
@@ -117,12 +120,13 @@
 
     inner_dev = quad_dev(half, 1 - core)
     outer_dev = (group, jnp.where(at_end, tile, jnp.where(core == 0, tile - 3, tile + 3)))
-    line_dev = quad_dev(1 - half, core)
     before_dev = (jnp.where(first, 1 - group, group), jnp.where(first, 0, tile - 1))
     after_dev = (jnp.where(final, 1 - group, group), jnp.where(final, last, tile + 1))
     side_dev = (before_dev, after_dev)
     side_slot = (jnp.where(first, 0, 1), jnp.where(final, 1, 0))
     here = pl.ds(pl.multiple_of(half * HALF, HALF), HALF)
+    held = pl.ds(pl.multiple_of(half * (HALF - SPARE), SPARE), HELD)
+    core_lines = pl.ds(pl.multiple_of(half * SPARE, SPARE), HALF)
 
     loads = [
         pltpu.make_async_copy(source, target, load_sem.at[i])
@@ -138,7 +142,7 @@
     def greet(dev):
         pl.semaphore_signal(barrier, inc=1, device_id=dev, device_id_type=MESH)
 
-    greeted = [inner_dev, line_dev, quad_dev(1 - half, 1 - core), x_dev(1), x_dev(3), y_dev(1), y_dev(3), z_dev(-1), z_dev(1)]
+    greeted = [inner_dev, quad_dev(1 - half, core), quad_dev(1 - half, 1 - core), x_dev(1), x_dev(3), y_dev(1), y_dev(3), z_dev(-1), z_dev(1)]
     for dev in greeted:
         greet(dev)
     home_beside = jnp.logical_and(outer_home, within)
@@ -173,10 +177,10 @@
     slot = jnp.where(outer_home, 0, 1)
 
     def move_copy(f, h):
-        return remote(sources[f].at[pl.ds(h * HALF, HALF)], moved.at[f, slot], move_send.at[f, h], move_recv.at[f, slot], quad_dev(h, half))
+        return remote(sources[f].at[pl.ds(h * (HALF - SPARE), HELD)], moved.at[f, slot], move_send.at[f, h], move_recv.at[f, slot], quad_dev(h, half))
 
     def own_copy(f):
-        return pltpu.make_async_copy(sources[f].at[here], moved.at[f, 0], move_own.at[f])
+        return pltpu.make_async_copy(sources[f].at[held], moved.at[f, 0], move_own.at[f])
 
     def move(f):
         for h in range(2):
@@ -214,10 +218,7 @@
         return remote(rows.at[0], near.at[s, c, 0], out_send.at[s, c, 0], out_recv.at[s, c, 0], outer_dev)
 
     def end_copy(s, c, rows, h):
-        return remote(rows.at[0], partner.at[s, c, here], out_send.at[s, c, h], out_recv.at[s, c, half], partner_dev(h))
-
-    def line_copy(s, c):
-        return remote(line_out.at[s, c], line_in.at[s, c], line_send.at[s, c], line_recv.at[s, c], line_dev)
+        return remote(rows.at[0, core_lines], partner.at[s, c, here], out_send.at[s, c, h], out_recv.at[s, c, half], partner_dev(h))
 
     def give(s, c, rows):
         @pl.when(within)
@@ -229,8 +230,6 @@
             for h in range(2):
                 end_copy(s, c, rows, h).start()
 
-        line_out[s, c] = jnp.where(half == 0, rows[:, HALF - 1 : HALF, :], rows[:, 0:1, :])
-        line_copy(s, c).start()
         in_copy(s, c, rows).start()
 
     def given(s, c, rows):
@@ -243,12 +242,10 @@
             for h in range(2):
                 end_copy(s, c, rows, h).wait_send()
 
-        line_copy(s, c).wait_send()
         in_copy(s, c, rows).wait_send()
 
     def take(s, c):
         arrived(near.at[s, c, 1], in_recv.at[s, c])
-        arrived(line_in.at[s, c], line_recv.at[s, c])
 
         @pl.when(within)
         def _():
@@ -259,18 +256,18 @@
             for h in range(2):
                 arrived(partner.at[s, c, pl.ds(h * HALF, HALF)], out_recv.at[s, c, h])
             near[s, c, 0] = jnp.dot(
-                onehot[here, :], partner[s, c], precision=lax.Precision.HIGHEST, preferred_element_type=jnp.float32
+                onehot[held, :], partner[s, c], precision=lax.Precision.HIGHEST, preferred_element_type=jnp.float32
             )
 
     def back_copy(a, rows, p):
         return remote(
-            rows.at[p], home.at[a, here], back_send.at[a, p], back_recv.at[a, half], quad_dev(core, (core, 1 - core)[p])
+            rows.at[p, core_lines], home.at[a, here], back_send.at[a, p], back_recv.at[a, half], quad_dev(core, (core, 1 - core)[p])
         )
 
     def give_back(a, rows):
         @pl.when(outer_home)
         def _():
-            home[a, here, :] = rows[0]
+            home[a, here, :] = rows[0, core_lines, :]
 
         @pl.when(jnp.logical_not(outer_home))
         def _():
@@ -301,8 +298,8 @@
         for dev in devs:
             pl.semaphore_signal(know.at[round_], inc=1, device_id=dev, device_id_type=MESH)
 
-    def hear(round_):
-        pl.semaphore_wait(know.at[round_], 2)
+    def hear(round_, count):
+        pl.semaphore_wait(know.at[round_], count)
 
     tell(0, (z_dev(-1), z_dev(1)))
     tell(Z_ROUNDS, (x_dev(1), x_dev(3)))
@@ -330,6 +327,8 @@
         DIFFUSION * (other[0] + other[1] + other[2] + other[3] - 6.0 * own)
         + 0.5 * (vel[1] * (other[0] - other[1]) + vel[2] * (other[2] - other[3]))
     )
+    hear(0, 2)
+    tell(1, (z_dev(-2), z_dev(2)))
     for side in range(2):
         arrived(beside.at[side], temp_recv.at[side])
 
@@ -341,16 +340,21 @@
     adj[...] = adj[...] + TIME_STEP * (DIFFUSION * (after + before) + 0.5 * (vel[0] * (after - before)))
     right[...] = forc[COMPS - 1] + BUOYANCY * adj[...]
     move(3)
-    adj_store = pltpu.make_async_copy(adj, adj_out, store_sem.at[2])
+    adj_store = pltpu.make_async_copy(adj, adj_out, store_sem.at[2 * COMPS])
     adj_store.start()
-    hear(0)
-    tell(1, (z_dev(-2), z_dev(2)))
+    hear(1, 2)
+    tell(2, (z_dev(-4), z_dev(4)))
+    hear(Z_ROUNDS, 2)
+    hear(Z_ROUNDS + 1, 2)
+    tell(Z_ROUNDS + 2, (y_dev(2), y_dev(1), y_dev(3)))
 
     moves = ((1, 1), (-1, 1), (1, 2), (-1, 2))
-    shape = (2, HALF, NR)
+    shape = (2, HELD, NR)
     y_place = lax.broadcasted_iota(jnp.int32, shape, 1)
     r_place = lax.broadcasted_iota(jnp.int32, shape, 2)
-    inside = (y_place < HALF - 1, y_place > 0, r_place < NR - 1, r_place > 0)
+    inside = (y_place < HELD - 1, y_place > 0, r_place < NR - 1, r_place > 0)
+    spare_at = (1 - half) * HALF
+    counts = jnp.logical_or(y_place < spare_at, y_place >= spare_at + SPARE)
     move_done(0)
     visc = moved.at[0]
     give(ITERS, 0, visc)
@@ -365,26 +369,28 @@
         weights[4, p] = between
     diag[...] = local + weights[4]
     take(ITERS, 0)
-    border = line_in[ITERS, 0]
-    for at, (place, own_half) in enumerate(((HALF - 1, 0), (0, 1))):
-        rows = slice(place, place + 1)
-        weight = jnp.where(half == own_half, 0.5 * (visc[:, rows, :] + border), 0.0)
-        diag[:, rows, :] = diag[:, rows, :] + weight
-        far[at] = weight
     outside = 0.5 * (visc[...] + near[ITERS, 0])
     diagonal = diag[...] + outside
     diag[...] = diagonal
+    measure[...] = jnp.where(counts, diagonal, 0.0)
     inverse_diagonal = 1.0 / diagonal
     weights[5] = outside * inverse_diagonal
     for k in range(5):
         weights[k] = weights[k] * inverse_diagonal
-    for at, place in enumerate((HALF - 1, 0)):
-        far[at] = far[at] * inverse_diagonal[:, place : place + 1, :]
-
     for c in range(COMPS):
+        if c + 1 == COMPS:
+            hear(2, 2)
+            tell(3, (z_dev(-8), z_dev(8)))
         move_done(1 + c)
         vs[0, c] = moved[1 + c] / diag[...]
         give(0, c, vs.at[0, c])
+
+    end_quad = jnp.logical_or(quad == 0, quad == last // 4)
+
+
+    @pl.when(jnp.logical_not(end_quad))
+    def _():
+        give_back(0, diag)
 
     mu = []
     for step in range(ITERS):
@@ -397,33 +403,40 @@
             for k, (move_by, axis) in enumerate(moves):
                 part = part + weights[k] * shift(value, move_by, axis)
             vs[step + 1, c] = part
-        mu.append(total_of(diag[...] * sum(vs[step, c] * vs[step, c] for c in range(COMPS))))
+        mu.append(total_of(measure[...] * sum(vs[step, c] * vs[step, c] for c in range(COMPS))))
+        odd = None
         for c in range(COMPS):
             take(step, c)
             vs[step + 1, c] = vs[step + 1, c] + weights[5] * near[step, c]
-            for at, place in enumerate((HALF - 1, 0)):
-                rows = slice(place, place + 1)
-                vs[step + 1, c, :, rows, :] = vs[step + 1, c, :, rows, :] + far[at] * line_in[step, c]
             if step + 1 < ITERS:
                 give(step + 1, c, vs.at[step + 1, c])
-        mu.append(total_of(diag[...] * sum(vs[step, c] * vs[step + 1, c] for c in range(COMPS))))
+            term = vs[step, c] * vs[step + 1, c]
+            odd = term if odd is None else odd + term
+        mu.append(total_of(measure[...] * odd))
         if step + 1 < ITERS:
             if step == 0:
-                give_back(0, diag)
-                hear(Z_ROUNDS)
-                hear(Z_ROUNDS + 1)
-            for c in range(COMPS):
-                give_back(1 + step * COMPS + c, vs.at[step + 1, c])
-            hear(1 + step)
-            tell(2 + step, (z_dev(-(4 << step)), z_dev(4 << step)))
+                hear(Z_ROUNDS + 2, 3)
+                tell(Z_ROUNDS + 3, (inner_dev,))
+
+            if step == 0:
+
+                @pl.when(jnp.logical_not(end_quad))
+                def _():
+                    for c in range(COMPS):
+                        give_back(1 + c, vs.at[1, c])
+
+            if step:
+
+                @pl.when(jnp.logical_not(end_quad))
+                def _():
+                    for c in range(COMPS):
+                        give_back(1 + COMPS + c, vs.at[2, c])
+
+                hear(Z_ROUNDS - 1, 2)
+                tell(Z_ROUNDS + 4, (inner_dev,))
 
     def small_copy(i, buffer, slot, dev):
         return remote(mine, buffer.at[slot], small_send.at[i], small_recv.at[i], dev)
-
-    def spread(i, buffer, slot, devs):
-        buffer[slot] = mine[...]
-        for dev in devs:
-            small_copy(i, buffer, slot, dev).start()
 
     def gather(i, buffer, count):
         part = buffer.at[pl.ds(0, count)]
@@ -433,38 +446,53 @@
         mine[...] = jnp.sum(buffer[...], axis=0)
 
     mine[...] = lane_row(mu)
-    hear(Z_ROUNDS - 1)
-    zbuf[z] = mine[...]
+    hear(Z_ROUNDS + 4, 1)
 
     def z_send(i, carry):
         k = (i + 1) // 2
         offset = NZ_CHIPS // 2 + k * (1 - 2 * lax.rem(i, 2))
-        small_copy(3, zbuf, z, z_dev(offset)).start()
+        dev = device_at(x, y, lax.rem(z + offset, NZ_CHIPS), 1 - core)
+        small_copy(0, zbuf, z, dev).start()
         return carry
 
-    lax.fori_loop(0, NZ_CHIPS - 1, z_send, 0)
+    lax.fori_loop(0, NZ_CHIPS, z_send, 0)
+
+    @pl.when(end_quad)
+    def _():
+        give_back(0, diag)
+        for c in range(COMPS):
+            give_back(1 + c, vs.at[1, c])
+            give_back(1 + COMPS + c, vs.at[2, c])
+
     for c in range(COMPS):
-        give_back(1 + (ITERS - 1) * COMPS + c, vs.at[ITERS, c])
-    gather(3, zbuf, NZ_CHIPS - 1)
-    spread(0, cbuf, core, [inner_dev])
-    gather(0, cbuf, 1)
-    spread(1, xbuf, x, [x_dev(2), x_dev(1), x_dev(3)])
-    gather(1, xbuf, NX_CHIPS - 1)
-    spread(2, ybuf, y, [y_dev(2), y_dev(1), y_dev(3)])
+        give_back(1 + 2 * COMPS + c, vs.at[3, c])
+    hear(Z_ROUNDS + 3, 1)
+    gather(0, zbuf, NZ_CHIPS)
+    plane_slot = (y * NX_CHIPS + x) * 2 + core
+    plane[plane_slot] = mine[...]
+
+    def plane_send(i, carry):
+        k = PLANE - 1 - i
+        dev = device_at(x ^ lax.rem(k // 2, NX_CHIPS), y ^ (k // (2 * NX_CHIPS)), z, core ^ lax.rem(k, 2))
+        small_copy(1, plane, plane_slot, dev).start()
+        return carry
+
+    lax.fori_loop(0, PLANE - 1, plane_send, 0)
     for a in range(1 + ITERS * COMPS):
         back_done(a)
-    gather(2, ybuf, NY_CHIPS - 1)
+    gather(1, plane, PLANE - 1)
     sums = mine[...]
     place, rest = gradient_coefficients([sums[:, k : k + 1] for k in range(MOMENTS)])
+    stores = [adj_store]
     for c in range(COMPS):
         full = forc[c] if c + 1 < COMPS else right[...]
         krylov = [full / home[0]] + [home[1 + step * COMPS + c] for step in range(ITERS)]
         sol[0, c] = sum(place[k] * krylov[k] for k in range(ITERS))
         sol[1, c] = rest[0] * full + home[0] * sum(rest[k] * krylov[k] for k in range(1, ITERS + 1))
-    sol_store = pltpu.make_async_copy(sol.at[0], sol_out, store_sem.at[0])
-    sol_store.start()
-    res_store = pltpu.make_async_copy(sol.at[1], res_out, store_sem.at[1])
-    res_store.start()
+        for at, out in enumerate((sol_out, res_out)):
+            store = pltpu.make_async_copy(sol.at[at, c], out.at[c], store_sem.at[at * COMPS + c])
+            store.start()
+            stores.append(store)
 
     for side in range(2):
         temp_copy(side).wait_send()
@@ -476,24 +504,23 @@
         for c in range(COMPS):
             given(s, c, vs.at[s, c])
             back_sent(1 + s * COMPS + c, vs.at[s + 1, c])
-    adj_store.wait()
-    sol_store.wait()
-    res_store.wait()
+    for store in stores:
+        store.wait()
 
 
 def body(adjoint_temp, misfit, viscosity, velocity, forcing, edge_table, pole_table):
     row = (NY, NR)
     rows = (COMPS, NY, NR)
-    pair = (2, HALF, NR)
+    pair = (2, HELD, NR)
     f32 = jnp.float32
     dma = pltpu.SemaphoreType.DMA
     any_space = pl.BlockSpec(memory_space=pl.ANY)
     sol, res, adj = pl.pallas_call(
         functools.partial(kernel, lax.axis_size("tile") - 1),
         out_shape=(
-            jax.ShapeDtypeStruct(rows, f32),
-            jax.ShapeDtypeStruct(rows, f32),
-            jax.ShapeDtypeStruct(row, f32),
+            pltpu.VMEM(rows, f32),
+            pltpu.VMEM(rows, f32),
+            pltpu.VMEM(row, f32),
         ),
         in_specs=[any_space] * 7,
         out_specs=(any_space,) * 3,
@@ -507,24 +534,20 @@
             pltpu.VMEM((1 + COMPS, *pair), f32),
             pltpu.VMEM((ITERS + 1, COMPS, *pair), f32),
             pltpu.VMEM((ITERS + 1, COMPS, *row), f32),
-            pltpu.VMEM((ITERS + 1, COMPS, 2, 1, NR), f32),
-            pltpu.VMEM((ITERS + 1, COMPS, 2, 1, NR), f32),
             pltpu.VMEM((ITERS + 1, COMPS, *pair), f32),
             pltpu.VMEM((6, *pair), f32),
-            pltpu.VMEM((2, 2, 1, NR), f32),
+            pltpu.VMEM(pair, f32),
             pltpu.VMEM(pair, f32),
             pltpu.VMEM(row, f32),
             pltpu.VMEM(row, f32),
             pltpu.VMEM((1 + ITERS * COMPS, *row), f32),
             pltpu.VMEM((2, *rows), f32),
             pltpu.VMEM((NY, NY), f32),
-            pltpu.VMEM((NX_CHIPS, 1, NR), f32),
-            pltpu.VMEM((NY_CHIPS, 1, NR), f32),
             pltpu.VMEM((NZ_CHIPS, 1, NR), f32),
-            pltpu.VMEM((2, 1, NR), f32),
+            pltpu.VMEM((PLANE, 1, NR), f32),
             pltpu.VMEM((1, NR), f32),
             dma((6,)),
-            dma((3,)),
+            dma((1 + 2 * COMPS,)),
             dma((2,)),
             dma((2,)),
             dma((1 + COMPS, 2)),
@@ -534,13 +557,11 @@
             dma((ITERS + 1, COMPS)),
             dma((ITERS + 1, COMPS, 2)),
             dma((ITERS + 1, COMPS, 2)),
-            dma((ITERS + 1, COMPS)),
-            dma((ITERS + 1, COMPS)),
             dma((1 + ITERS * COMPS, 2)),
             dma((1 + ITERS * COMPS, 2)),
-            dma((4,)),
-            dma((4,)),
-            pltpu.SemaphoreType.REGULAR((Z_ROUNDS + 2,)),
+            dma((2,)),
+            dma((2,)),
+            pltpu.SemaphoreType.REGULAR((Z_ROUNDS + 5,)),
         ],
         compiler_params=pltpu.CompilerParams(collective_id=0, has_side_effects=True, vmem_limit_bytes=60 << 20),
     )(

time: 75.3 us -> 70 us (0.930); the launches traced: 74.2 us -> 69.8 us
  Pallas kernels: 70 us -> 67 us
  local copies, waits for them, and re-layouts: 3.5 us -> 2.15 us
    pallas_call x1, Pallas kernels: 70 us -> 67 us  [body(): pl.pallas_call(functools.partial(kernel, lax.axis_size('tile') - 1), out_...]
    unnamed x7 -> x3, local copies, waits for them, and re-layouts: 3.5 us -> 2.15 us
where the time goes in v3:
time: 70 us; the launch traced here: 69.8 us
  Pallas kernels  67 us (96%)
  local copies, waits for them, and re-layouts  2.15 us (3%)
    pallas_call x1, Pallas kernels, body(): pl.pallas_call(functools.partial(kernel, lax.axis_size('tile') - 1), out_...  67 us
    unnamed x3, local copies, waits for them, and re-layouts  2.15 us

profile of v3, /device:TPU:1, one launch (start us, length us, event | category | flops | bytes accessed | tf_op | source)
XLA Modules:
  0.0 69.8 jit_solution(10282247513901681037)
XLA Ops:
  0.6 67.0 %shard_map.94 = (f32[3,256,128]{2,1,0:T(8,128)S(1)}, f32[3,256,128]{2,1,0:T(8,128)S(1)}, f32[256,128]{1,0:T(8,128)S(1)}) custom-call(f32[256,128]{1,0:T(8,128)} %bitcast.17, f32[256,128]{1,0:T(8,128)} %bitcast.18, f32[256,128]{1,0:T(8,128)} %bitcast.19, f32[3,256,128]{2,1,0:T(8,128)} %bitcast.15, f32[3,256,128]{2,1,0:T(8,128)} %bitcast.16, ...), custom_call_target="tpu_custom_call" | custom-call | tf_op jit(solution)/shard_map/pallas_call | solution.py:518
  67.7 0.7 %copy.15 = f32[3,1,1,256,128]{4,3,2,1,0:T(8,128)} copy(f32[3,1,1,256,128]{4,3,2,1,0:T(8,128)S(1)} %bitcast.13) | data formatting | bytes 786432
  68.4 0.7 %copy.16 = f32[3,1,1,256,128]{4,3,2,1,0:T(8,128)} copy(f32[3,1,1,256,128]{4,3,2,1,0:T(8,128)S(1)} %bitcast.12) | data formatting | bytes 786432
  69.2 0.7 copy.17

commit v4 on v3

--- a/solution.py
+++ b/solution.py
@@ -480,13 +480,15 @@
     lax.fori_loop(0, PLANE - 1, plane_send, 0)
     for a in range(1 + ITERS * COMPS):
         back_done(a)
+    for c in range(COMPS):
+        vel[c] = (forc[c] if c + 1 < COMPS else right[...]) / home[0]
     gather(1, plane, PLANE - 1)
     sums = mine[...]
     place, rest = gradient_coefficients([sums[:, k : k + 1] for k in range(MOMENTS)])
     stores = [adj_store]
     for c in range(COMPS):
         full = forc[c] if c + 1 < COMPS else right[...]
-        krylov = [full / home[0]] + [home[1 + step * COMPS + c] for step in range(ITERS)]
+        krylov = [vel[c]] + [home[1 + step * COMPS + c] for step in range(ITERS)]
         sol[0, c] = sum(place[k] * krylov[k] for k in range(ITERS))
         sol[1, c] = rest[0] * full + home[0] * sum(rest[k] * krylov[k] for k in range(1, ITERS + 1))
         for at, out in enumerate((sol_out, res_out)):

time: 70 us -> 69.9 us (level)
  no operation moved by 1% of the time
where the time goes in v4:
time: 69.9 us; the launch traced here: 69.8 us
  Pallas kernels  67 us (96%)
  local copies, waits for them, and re-layouts  2.15 us (3%)
    pallas_call x1, Pallas kernels, body(): pl.pallas_call(functools.partial(kernel, lax.axis_size('tile') - 1), out_...  67 us
    unnamed x3, local copies, waits for them, and re-layouts  2.15 us

profile of v4, /device:TPU:1, one launch (start us, length us, event | category | flops | bytes accessed | tf_op | source)
XLA Modules:
  0.0 69.8 jit_solution(4112827067675497296)
XLA Ops:
  0.6 67.0 %shard_map.94 = (f32[3,256,128]{2,1,0:T(8,128)S(1)}, f32[3,256,128]{2,1,0:T(8,128)S(1)}, f32[256,128]{1,0:T(8,128)S(1)}) custom-call(f32[256,128]{1,0:T(8,128)} %bitcast.17, f32[256,128]{1,0:T(8,128)} %bitcast.18, f32[256,128]{1,0:T(8,128)} %bitcast.19, f32[3,256,128]{2,1,0:T(8,128)} %bitcast.15, f32[3,256,128]{2,1,0:T(8,128)} %bitcast.16, ...), custom_call_target="tpu_custom_call" | custom-call | tf_op jit(solution)/shard_map/pallas_call | solution.py:520
  67.7 0.7 %copy.15 = f32[3,1,1,256,128]{4,3,2,1,0:T(8,128)} copy(f32[3,1,1,256,128]{4,3,2,1,0:T(8,128)S(1)} %bitcast.13) | data formatting | bytes 786432
  68.4 0.7 %copy.16 = f32[3,1,1,256,128]{4,3,2,1,0:T(8,128)} copy(f32[3,1,1,256,128]{4,3,2,1,0:T(8,128)S(1)} %bitcast.12) | data formatting | bytes 786432
  69.1 0.7 copy.17
